TPU v7x, 512 devices: a whole 4x4x16 slice. The times are simulated.
512 devices in a mesh: fsdp: 32 (over z, y_lo), head: 4 (over y_hi, core), rep: 4 (over x).
Axes of the slice: x: 4, y: 4 (y_hi: 2, y_lo: 2; y = y_hi * 2 + y_lo), z: 16, core: 2. Of those that a mesh axis runs over, the one named last changes fastest.
Arguments:
- query_up: bfloat16 [4, 1536, 64, 192], P('rep', 'fsdp', 'head'), may hold values from -1.796875 to 1.796875
- latent_up: bfloat16 [4, 512, 64, 256], P('rep', 'fsdp', 'head'), may hold values from -1.796875 to 1.796875
- latent_gain: float32 [4, 512], P('rep'), may hold values from 0.3 to 3
- server_heads: int32 [64], replicated, may hold values from 0 to 63, as said below
Outputs:
- absorbed: bfloat16 [4, 64, 1536, 512], P(None, 'head', 'fsdp')
Inputs may be any that keep to these rules, and one draw needn't show every extreme that they name: `server_heads`: A permutation of the 64 heads. Slots o * 16 to (o + 1) * 16 - 1 belong to owner o; slot o * 16 + b * 4 + j, for j < 4, holds a head of block b, the heads b * 16 to (b + 1) * 16 - 1.
All inputs are finite; a program needn't handle non-finite values.
Results may differ from a plain program's by a relative error of at most 0.012.
Values may be sent and summed in bfloat16 or wider, within the bound.
A program may use at most 64 MiB of HBM per device.

v0:
```python
import jax
import jax.numpy as jnp
from jax import lax
from jax.sharding import PartitionSpec as P

NOPE = 128


def absorb_heads(query_nope, key_nope, gain_rows):
    product = jnp.einsum(
        "lrhd,lchd->lhrc",
        query_nope,
        lax.all_gather(key_nope, "fsdp", axis=1, tiled=True),
        preferred_element_type=jnp.float32,
    )
    return (product * gain_rows[:, None, None, :]).astype(jnp.bfloat16)


def local(query_up, latent_up, latent_gain, server_heads):
    owners = lax.axis_size("head")
    block = lax.axis_index("head")
    local_heads = query_up.shape[2]
    quota = local_heads // owners
    width = NOPE
    owner_table = server_heads.reshape(owners, owners, quota)
    local_order = (
        lax.dynamic_index_in_dim(owner_table, block, 1, keepdims=False) - block * local_heads
    ).reshape(-1)
    query_nope = query_up[:, :, :, :width]
    key_nope = latent_up[:, :, :, :width]
    matrices = absorb_heads(query_nope, key_nope, latent_gain)
    layers_here = matrices.shape[0]
    sorted_blocks = jnp.take(matrices, local_order, axis=1)
    sorted_blocks = sorted_blocks.reshape(
        layers_here, owners, quota, matrices.shape[2], matrices.shape[3]
    )
    moved = lax.all_to_all(sorted_blocks, "head", split_axis=1, concat_axis=1, tiled=True)
    matrices = moved.reshape(layers_here, local_heads, matrices.shape[2], matrices.shape[3])
    matrices = lax.all_gather(matrices, "rep", axis=0, tiled=True)
    return matrices


def solution(mesh):
    in_specs = (P("rep", "fsdp", "head", None), P("rep", "fsdp", "head", None), P("rep", None), P())
    out_specs = P(None, "head", "fsdp", None)
    return jax.shard_map(local, mesh=mesh, in_specs=in_specs, out_specs=out_specs, check_vma=False)
```

profile of v0, /device:TPU:1, one launch (start us, length us, event | category | flops | bytes accessed | tf_op | source)
XLA Modules:
  0.0 222.9 jit_solution(12069933514380016635)
XLA Ops:
  6.5 0.0 all-gather.3.cloned.1.call-start
  6.5 0.8 slice.7
  7.4 0.6 copy.11
  8.0 0.0 all-gather.3.cloned.1.call-update
  8.1 0.0 all-gather.5.cloned.1.call-start
  8.1 0.7 reshape.64
  8.9 0.5 broadcast.78
  9.4 0.6 fusion.5
  10.0 0.1 sub.26
  10.1 0.9 slice.6
  11.1 116.4 %all-gather.3.cloned.1.call-done = bf16[1,512,16,128]{3,1,2,0:T(8,128)(2,1)} async-done(((bf16[1,16,16,128]{3,1,2,0:T(8,128)(2,1)}), bf16[1,512,16,128]{3,1,2,0:T(8,128)(2,1)}) %all-gather.3.cloned.1.call-update) | async-done | bytes 2097168 | tf_op jit(solution)/shard_map/all_gather | solution.py:13
  127.5 2.4 %multiply_convert_fusion = bf16[16,48,512]{2,1,0:T(8,128)(2,1)S(1)} fusion(bf16[1,512,16,128]{3,1,2,0:T(8,128)(2,1)} %all-gather.3.cloned.1.call-done, f32[512]{0:T(512)} %bitcast.19, bf16[1,48,16,128]{3,2,1,0:T(8,128)(2,1)S(1)} %slice.6), kind=kOutput, calls=%fused_computation.3 | convolution fusion | flops 101449728 | bytes 3082240 | tf_op jit(solution)/shard_map/lrhd,lchd->lhrc/dot_general | solution.py:10
  130.0 0.6 gather_fusion
  130.6 0.1 broadcast_select_fusion
  130.7 39.4 %all_to_all.5 = bf16[1,4,4,48,512]{4,3,2,0,1:T(8,128)(2,1)} all-to-all(bf16[1,4,4,48,512]{4,3,2,0,1:T(8,128)(2,1)S(1)} %broadcast_select_fusion), channel_id=1, replica_groups=mesh['fsdp'=32,'head'=4,'rep'=4] {'head'}, dimensions={1} | all-to-all | bytes 1572864 | tf_op jit(solution)/shard_map/all_to_all | solution.py:37
  170.1 0.0 all-gather.5.cloned.1.call-update
  170.1 42.2 %all-gather.5.cloned.1.call-done = bf16[4,16,48,512]{3,2,1,0:T(8,128)(2,1)} async-done(((bf16[1,16,48,512]{3,2,1,0:T(8,128)(2,1)}), bf16[4,16,48,512]{3,2,1,0:T(8,128)(2,1)}) %all-gather.5.cloned.1.call-update) | async-done | bytes 3145744 | tf_op jit(solution)/shard_map/all_gather | solution.py:39
  212.3 3.8 %copy.15 = bf16[4,16,48,512]{3,2,1,0:T(8,128)(2,1)} copy(bf16[4,16,48,512]{3,2,1,0:T(8,128)(2,1)} %all-gather.5.cloned.1.call-done) | data formatting | bytes 6291456
  (3 shorter events, 0.0 us)
Async XLA Ops:
  6.5 121.0 %all-gather.3.cloned.1.call-start = ((), (), s32[]{:S(2)}) async-start(), calls=%async_computation.1 | async-start | bytes 2162688 | tf_op jit(solution)/shard_map/all_gather | solution.py:13
  8.1 204.3 %all-gather.5.cloned.1.call-start = ((), (), s32[]{:S(2)}) async-start(), calls=%async_computation.2 | async-start | bytes 3932160 | tf_op jit(solution)/shard_map/all_gather | solution.py:39
Sparse Core Ops, SparseCore 0:
  9.4 118.1 all-gather.2
  170.2 42.0 all-gather.4
where the time goes:
time: 223 us
  waiting for transfers between devices  159 us (71%)
  blocking collectives  39.4 us (18%)
  between operations  13.5 us (6%)
  local copies, waits for them, and re-layouts  8.17 us (4%)
  matrix products  2.43 us (1%)
    all_gather x1, waiting for transfers between devices, absorb_heads(): lax.all_gather(key_nope, 'fsdp', axis=1, tiled=True)  116 us
    all_gather x1, waiting for transfers between devices, local(): matrices = lax.all_gather(matrices, 'rep', axis=0, tiled=True)  42.2 us
    all_to_all x1, blocking collectives, local(): lax.all_to_all(sorted_blocks, 'head', split_axis=1, concat_axis=1, tiled=...  39.4 us
  transfers between devices with their start and end apart: 2, of which 2 were waited for; matrix products, arithmetic and copies ran while one was open for 1% of the time, Pallas kernels for 0%

commit v1 on v0

v1 whole, which is shorter than its diff:
```python
import jax
import jax.numpy as jnp
from jax import lax
from jax.experimental import pallas as pl
from jax.experimental.pallas import tpu as pltpu
from jax.sharding import PartitionSpec as P

MESH = pl.DeviceIdType.MESH
NOPE = 128
NZ = 16
LEGS = {1: (1,), 3: (1, 2), 6: (1, 2), -1: (-1,), -3: (-1,), -5: (-1, -2)}
FIRST = tuple(LEGS)
LAST = sum(len(v) for v in LEGS.values())
SPANS = sorted({abs(o) for o in FIRST} | {abs(s) for v in LEGS.values() for s in v})


def kernel(q_hbm, k_hbm, gain_ref, heads_ref, out_ref,
           q_in, k_in, q_f32, k_f32, q_send, k_send, q_all, k_all, prod,
           in_sem, ex_send, ex_recv, z_send, z_first, z_last, y_send, y_recv, x_send, x_recv, f_recv):
    f, b, x = lax.axis_index("fsdp"), lax.axis_index("head"), lax.axis_index("rep")
    z, yl, yh, c = f // 2, f % 2, b // 2, b % 2
    layers = lax.axis_size("rep")
    rows, cols = q_in.shape[0], k_in.shape[0]
    heads = q_in.shape[1]
    steps = heads // 2

    def device(zz=None, yy=None, hh=None, xx=None):
        return {
            "fsdp": (z if zz is None else zz) * 2 + (yl if yy is None else yy),
            "head": b if hh is None else hh,
            "rep": x if xx is None else xx,
        }

    def along_z(offset):
        return (z + offset + 2 * NZ) % NZ

    x_up, x_down = (x + 1) % layers, (x + layers - 1) % layers

    def owner(k):
        return (yh + k // 2) % 2 * 2 + (c + k % 2) % 2

    partners = [device(zz=along_z(s * v)) for v in SPANS for s in (1, -1)]
    partners += [device(xx=x_up), device(xx=x_down)]
    partners += [device(yy=(yl + e) % 2, hh=owner(k)) for k in range(4) for e in range(2) if (k, e) != (0, 0)]
    barrier = pltpu.get_barrier_semaphore()
    for p in partners:
        pl.semaphore_signal(barrier, inc=1, device_id=p, device_id_type=MESH)

    q_copy = pltpu.make_async_copy(q_hbm.at[0, :, :, pl.ds(0, NOPE)], q_in, in_sem.at[0])
    k_copy = pltpu.make_async_copy(k_hbm.at[0, :, :, pl.ds(0, NOPE)], k_in, in_sem.at[1])
    k_copy.start()
    q_copy.start()
    k_copy.wait()
    k_f32[...] = k_in[...].reshape(cols * heads, NOPE).astype(jnp.float32)
    my_rows = pl.ds(pl.multiple_of(z * 2 * cols + yl * cols, cols), cols)

    def head_of(t, half):
        return heads_ref[owner(t % 4) * heads + b * 4 + half * 2 + t // 4] % heads

    for t in range(steps):
        k_send[t] = k_f32[pl.ds(head_of(t, 1 - yl), cols, stride=heads), :].astype(jnp.bfloat16)
        k_all[t, my_rows, :] = k_f32[pl.ds(head_of(t, yl), cols, stride=heads), :].astype(jnp.bfloat16)
    q_copy.wait()
    q_f32[...] = q_in[...].reshape(rows * heads, NOPE).astype(jnp.float32)
    for t in range(steps):
        q_send[t] = q_f32[pl.ds(head_of(t, 1 - yl), rows, stride=heads), :].astype(jnp.bfloat16)
        q_all[t, yl] = q_f32[pl.ds(head_of(t, yl), rows, stride=heads), :].astype(jnp.bfloat16)

    pl.semaphore_wait(barrier, len(partners))

    mate = device(yy=1 - yl)

    def exchange(src, dst, i):
        return pltpu.make_async_remote_copy(
            src, dst, ex_send.at[i], ex_recv.at[i], device_id=mate, device_id_type=MESH)

    ex = [
        exchange(k_send.at[pl.ds(0, 1)], k_all.at[pl.ds(0, 1), my_rows], 0),
        exchange(k_send.at[pl.ds(1, steps - 1)], k_all.at[pl.ds(1, steps - 1), my_rows], 1),
        exchange(q_send, q_all.at[:, yl], 2),
    ]
    for e in ex:
        e.start()

    def slice_at(t, where):
        return k_all.at[t, pl.ds(pl.multiple_of(where * 2 * cols, 2 * cols), 2 * cols)]

    def z_copy(t, where, to, recv):
        ref = slice_at(t, where)
        return pltpu.make_async_remote_copy(
            ref, ref, z_send.at[t], recv, device_id=device(zz=to), device_id_type=MESH)

    def sign(t):
        return 1 - 2 * (t % 2)

    def first(t):
        for i, o in enumerate(FIRST):
            z_copy(t, z, along_z(sign(t) * o), z_first.at[t, i]).start()

    def relay(t):
        for i, o in enumerate(FIRST):
            origin = along_z(-sign(t) * o)
            z_copy(t, origin, z, z_first.at[t, i]).wait_recv()
            for s in LEGS[o]:
                z_copy(t, origin, along_z(sign(t) * s), z_last.at[t]).start()

    def y_copy(t, yy, hh, slot, half):
        return pltpu.make_async_remote_copy(
            prod.at[t, yy], out_ref.at[x, slot], y_send.at[t], y_recv.at[t, half],
            device_id=device(yy=yy, hh=hh), device_id_type=MESH)

    def multiply(t):
        pltpu.make_async_copy(
            k_all.at[t, pl.ds(0, LAST * 2 * cols)], k_all.at[t, pl.ds(0, LAST * 2 * cols)], z_last.at[t]).wait()
        product = lax.dot_general(
            q_all[t].reshape(2 * rows, NOPE), k_all[t], (((1,), (1,)), ((), ())),
            preferred_element_type=jnp.float32)
        prod[t] = (product * gain_ref[...]).astype(jnp.bfloat16).reshape(2, rows, product.shape[1])
        k = t % 4
        slot = b * 4 + yl * 2 + t // 4
        y_copy(t, 1 - yl, owner(k), slot, yl).start()

        @pl.when(k == 0)
        def _():
            out_ref[x, slot] = prod[t, yl]

        @pl.when(k != 0)
        def _():
            y_copy(t, yl, owner(k), slot, yl).start()

    def slot_of(t, half):
        return owner(t % 4) * 4 + half * 2 + t // 4

    def x_copy(layer, slot, to, t, recv):
        ref = out_ref.at[layer, slot]
        return pltpu.make_async_remote_copy(
            ref, ref, x_send.at[t], recv, device_id=device(xx=to), device_id_type=MESH)

    def spread(t):
        def both(half):
            slot = slot_of(t, half)
            x_copy(x, slot, x_up, t, x_recv.at[t, half, 0]).start()
            x_copy(x, slot, x_down, t, x_recv.at[t, half, 1]).start()

        @pl.when(t % 4 != 0)
        def _():
            y_copy(t, yl, b, 0, yl).wait_recv()

        both(yl)
        y_copy(t, yl, b, 0, 1 - yl).wait_recv()
        both(1 - yl)

    def forward(t):
        x_copy(x_down, slot_of(t, 0), x_up, t, x_recv.at[t, 0, 0]).wait_recv()
        x_copy(x_down, slot_of(t, 0), x_up, t, f_recv.at[t, 0]).start()
        x_copy(x_up, slot_of(t, 1), x_down, t, x_recv.at[t, 1, 1]).wait_recv()
        x_copy(x_up, slot_of(t, 1), x_down, t, f_recv.at[t, 1]).start()

    def collect(t):
        x_copy(x_up, slot_of(t, 0), x_up, t, x_recv.at[t, 0, 1]).wait_recv()
        x_copy(x_down, slot_of(t, 1), x_up, t, x_recv.at[t, 1, 0]).wait_recv()
        for half in range(2):
            x_copy((x + 2) % layers, slot_of(t, half), x_up, t, f_recv.at[t, half]).wait_recv()

    ex[0].wait_recv()
    first(0)
    ex[1].wait_recv()
    lax.fori_loop(1, steps, lambda t, _: (first(t), 0)[1], 0)
    ex[2].wait_recv()

    stages = ((relay, 0), (multiply, 3), (spread, 4), (forward, 6), (collect, 8))

    def turn(i, _):
        for stage, lag in stages:
            @pl.when((i >= lag) & (i < lag + steps))
            def _():
                stage(i - lag)
        return 0

    lax.fori_loop(0, steps + stages[-1][1], turn, 0)

    for e in ex:
        e.wait_send()

    def drain(t, _):
        pltpu.make_async_copy(
            k_all.at[t, pl.ds(0, (NZ - 1) * 2 * cols)], k_all.at[t, pl.ds(0, (NZ - 1) * 2 * cols)], z_send.at[t]).wait()
        y_copy(t, yl, b, 0, yl).wait_send()

        @pl.when(t % 4 != 0)
        def _():
            y_copy(t, yl, b, 0, yl).wait_send()

        pltpu.make_async_copy(
            out_ref.at[0, pl.ds(0, 6)], out_ref.at[0, pl.ds(0, 6)], x_send.at[t]).wait()
        return 0

    lax.fori_loop(0, steps, drain, 0)


def local(query_up, latent_up, latent_gain, server_heads):
    _, rows, heads, _ = query_up.shape
    cols = latent_up.shape[1]
    steps = heads // 2
    layers = lax.axis_size("rep")
    all_cols = latent_gain.shape[1]
    bf, dma = jnp.bfloat16, pltpu.SemaphoreType.DMA
    return pl.pallas_call(
        kernel,
        out_shape=jax.ShapeDtypeStruct((layers, heads, rows, all_cols), bf),
        in_specs=[
            pl.BlockSpec(memory_space=pl.ANY),
            pl.BlockSpec(memory_space=pl.ANY),
            pl.BlockSpec(memory_space=pltpu.VMEM),
            pl.BlockSpec(memory_space=pltpu.SMEM),
        ],
        out_specs=pl.BlockSpec(memory_space=pltpu.VMEM),
        scratch_shapes=[
            pltpu.VMEM((rows, heads, NOPE), bf),
            pltpu.VMEM((cols, heads, NOPE), bf),
            pltpu.VMEM((rows * heads, NOPE), jnp.float32),
            pltpu.VMEM((cols * heads, NOPE), jnp.float32),
            pltpu.VMEM((steps, rows, NOPE), bf),
            pltpu.VMEM((steps, cols, NOPE), bf),
            pltpu.VMEM((steps, 2, rows, NOPE), bf),
            pltpu.VMEM((steps, all_cols, NOPE), bf),
            pltpu.VMEM((steps, 2, rows, all_cols), bf),
            dma((2,)),
            dma((3,)),
            dma((3,)),
            dma((steps,)),
            dma((steps, len(FIRST))),
            dma((steps,)),
            dma((steps,)),
            dma((steps, 2)),
            dma((steps,)),
            dma((steps, 2, 2)),
            dma((steps, 2)),
        ],
        compiler_params=pltpu.CompilerParams(
            collective_id=0, has_side_effects=True, vmem_limit_bytes=48 << 20),
    )(query_up, latent_up, latent_gain, server_heads)


def solution(mesh):
    in_specs = (P("rep", "fsdp", "head", None), P("rep", "fsdp", "head", None), P("rep", None), P())
    out_specs = P(None, "head", "fsdp", None)
    return jax.shard_map(local, mesh=mesh, in_specs=in_specs, out_specs=out_specs, check_vma=False)
```

time: 223 us -> 72.7 us (0.33)
  waiting for transfers between devices: 159 us -> 0 us
  Pallas kernels: 0 us -> 67.5 us
  blocking collectives: 39.4 us -> 0 us
  between operations: 13.5 us -> 0.01 us
  local copies, waits for them, and re-layouts: 8.17 us -> 4.9 us
  matrix products: 2.43 us -> 0 us
    all_gather x2 -> x0, waiting for transfers between devices: 159 us -> none  [the longest x1 116 us: absorb_heads(): lax.all_gather(key_nope, 'fsdp', axis=1, tiled=True)]
    pallas_call x0 -> x1, Pallas kernels: none -> 67.5 us  [local(): pl.pallas_call(kernel, out_shape=jax.ShapeDtypeStruct((layers, heads, row...]
    all_to_all x1 -> x0, blocking collectives: 39.4 us -> none  [local(): lax.all_to_all(sorted_blocks, 'head', split_axis=1, concat_axis=1, tiled=...]
    dot_general x1 -> x0, matrix products: 2.43 us -> none  [absorb_heads(): jnp.einsum('lrhd,lchd->lhrc', query_nope, lax.all_gather(key_nope, 'fsdp'...]
    unnamed x2 -> x9, local copies, waits for them, and re-layouts: 4.42 us -> 4.9 us
  transfers between devices with their start and end apart: 2 -> 0, of which waited for: 2 -> 0; matrix products, arithmetic and copies ran while one was open for 1% -> 0% of each run, Pallas kernels for 0% -> 0%
where the time goes in v1:
time: 72.7 us; the launch traced here: 72.4 us
  Pallas kernels  67.5 us (93%)
  local copies, waits for them, and re-layouts  4.9 us (7%)
    pallas_call x1, Pallas kernels, local(): pl.pallas_call(kernel, out_shape=jax.ShapeDtypeStruct((layers, heads, row...  67.5 us
    unnamed x9, local copies, waits for them, and re-layouts  4.9 us

profile of v1, /device:TPU:1, one launch (start us, length us, event | category | flops | bytes accessed | tf_op | source)
XLA Modules:
  0.0 72.4 jit_solution(11672314358775680276)
XLA Ops:
  0.0 0.0 copy-start
  0.0 1.0 %copy-done = bf16[1,48,16,192]{3,2,1,0:T(8,128)(2,1)S(1)} copy-done((bf16[1,48,16,192]{3,2,1,0:T(8,128)(2,1)S(1)}, bf16[1,48,16,192]{3,2,1,0:T(8,128)(2,1)}, u32[]{:S(2)}) %copy-start) | copy-done | bytes 294936
  1.0 0.0 copy-start.1
  1.0 0.9 %copy-done.1 = bf16[1,16,16,256]{3,2,1,0:T(8,128)(2,1)S(1)} copy-done((bf16[1,16,16,256]{3,2,1,0:T(8,128)(2,1)S(1)}, bf16[1,16,16,256]{3,2,1,0:T(8,128)(2,1)}, u32[]{:S(2)}) %copy-start.1) | copy-done | bytes 131096
  1.9 0.0 copy-start.2
  1.9 0.7 copy-done.2
  2.6 0.0 copy-start.3
  2.6 0.7 copy-done.3
  3.2 67.5 %shard_map.46 = bf16[4,16,48,512]{3,2,1,0:T(8,128)(2,1)S(1)} custom-call(bf16[1,48,16,192]{3,2,1,0:T(8,128)(2,1)S(1)} %copy-done, bf16[1,16,16,256]{3,2,1,0:T(8,128)(2,1)S(1)} %copy-done.1, f32[1,512]{1,0:T(1,128)S(1)} %copy-done.2, s32[64]{0:T(128)S(1)} %copy-done.3), custom_call_target="tpu_custom_call" | custom-call | tf_op jit(solution)/shard_map/pallas_call | solution.py:208
  70.8 1.7 %copy.6 = bf16[4,16,48,512]{3,2,1,0:T(8,128)(2,1)} copy(bf16[4,16,48,512]{3,2,1,0:T(8,128)(2,1)S(1)} %shard_map.46) | data formatting | bytes 6291456
Async XLA Ops:
  0.0 1.0 %copy-start = (bf16[1,48,16,192]{3,2,1,0:T(8,128)(2,1)S(1)}, bf16[1,48,16,192]{3,2,1,0:T(8,128)(2,1)}, u32[]{:S(2)}) copy-start(bf16[1,48,16,192]{3,2,1,0:T(8,128)(2,1)} %q_hbm.1) | copy-start | bytes 884740
  1.0 0.9 %copy-start.1 = (bf16[1,16,16,256]{3,2,1,0:T(8,128)(2,1)S(1)}, bf16[1,16,16,256]{3,2,1,0:T(8,128)(2,1)}, u32[]{:S(2)}) copy-start(bf16[1,16,16,256]{3,2,1,0:T(8,128)(2,1)} %k_hbm.1) | copy-start | bytes 393220
  1.9 0.7 copy-start.2
  2.6 0.7 copy-start.3

commit v2 on v1

--- a/solution.py
+++ b/solution.py
@@ -8,15 +8,17 @@
 MESH = pl.DeviceIdType.MESH
 NOPE = 128
 NZ = 16
+AHEAD = 3
 LEGS = {1: (1,), 3: (1, 2), 6: (1, 2), -1: (-1,), -3: (-1,), -5: (-1, -2)}
 FIRST = tuple(LEGS)
 LAST = sum(len(v) for v in LEGS.values())
+REACH = sorted({abs(o) for o in FIRST})
 SPANS = sorted({abs(o) for o in FIRST} | {abs(s) for v in LEGS.values() for s in v})
 
 
-def kernel(q_hbm, k_hbm, gain_ref, heads_ref, out_ref,
-           q_in, k_in, q_f32, k_f32, q_send, k_send, q_all, k_all, prod,
-           in_sem, ex_send, ex_recv, z_send, z_first, z_last, y_send, y_recv, x_send, x_recv, f_recv):
+def kernel(q_hbm, k_hbm, gain_hbm, heads_hbm, out_ref,
+           gain_ref, heads_ref, q_in, k_in, q_f32, k_f32, q_send, k_send, q_all, k_all, prod,
+           in_sem, ex_send, ex_recv, z_send, z_mate, z_first, z_last, y_send, y_recv, x_send, x_recv, f_recv):
     f, b, x = lax.axis_index("fsdp"), lax.axis_index("head"), lax.axis_index("rep")
     z, yl, yh, c = f // 2, f % 2, b // 2, b % 2
     layers = lax.axis_size("rep")
@@ -40,17 +42,23 @@
         return (yh + k // 2) % 2 * 2 + (c + k % 2) % 2
 
     partners = [device(zz=along_z(s * v)) for v in SPANS for s in (1, -1)]
+    partners += [device(zz=along_z(s * v), yy=1 - yl) for v in REACH for s in (1, -1)]
     partners += [device(xx=x_up), device(xx=x_down)]
     partners += [device(yy=(yl + e) % 2, hh=owner(k)) for k in range(4) for e in range(2) if (k, e) != (0, 0)]
     barrier = pltpu.get_barrier_semaphore()
     for p in partners:
         pl.semaphore_signal(barrier, inc=1, device_id=p, device_id_type=MESH)
 
-    q_copy = pltpu.make_async_copy(q_hbm.at[0, :, :, pl.ds(0, NOPE)], q_in, in_sem.at[0])
-    k_copy = pltpu.make_async_copy(k_hbm.at[0, :, :, pl.ds(0, NOPE)], k_in, in_sem.at[1])
-    k_copy.start()
-    q_copy.start()
-    k_copy.wait()
+    copies = [
+        pltpu.make_async_copy(heads_hbm, heads_ref, in_sem.at[0]),
+        pltpu.make_async_copy(k_hbm.at[0, :, :, pl.ds(0, NOPE)], k_in, in_sem.at[1]),
+        pltpu.make_async_copy(q_hbm.at[0, :, :, pl.ds(0, NOPE)], q_in, in_sem.at[2]),
+        pltpu.make_async_copy(gain_hbm, gain_ref, in_sem.at[3]),
+    ]
+    for copy in copies:
+        copy.start()
+    copies[0].wait()
+    copies[1].wait()
     k_f32[...] = k_in[...].reshape(cols * heads, NOPE).astype(jnp.float32)
     my_rows = pl.ds(pl.multiple_of(z * 2 * cols + yl * cols, cols), cols)
 
@@ -60,27 +68,7 @@
     for t in range(steps):
         k_send[t] = k_f32[pl.ds(head_of(t, 1 - yl), cols, stride=heads), :].astype(jnp.bfloat16)
         k_all[t, my_rows, :] = k_f32[pl.ds(head_of(t, yl), cols, stride=heads), :].astype(jnp.bfloat16)
-    q_copy.wait()
-    q_f32[...] = q_in[...].reshape(rows * heads, NOPE).astype(jnp.float32)
-    for t in range(steps):
-        q_send[t] = q_f32[pl.ds(head_of(t, 1 - yl), rows, stride=heads), :].astype(jnp.bfloat16)
-        q_all[t, yl] = q_f32[pl.ds(head_of(t, yl), rows, stride=heads), :].astype(jnp.bfloat16)
-
     pl.semaphore_wait(barrier, len(partners))
-
-    mate = device(yy=1 - yl)
-
-    def exchange(src, dst, i):
-        return pltpu.make_async_remote_copy(
-            src, dst, ex_send.at[i], ex_recv.at[i], device_id=mate, device_id_type=MESH)
-
-    ex = [
-        exchange(k_send.at[pl.ds(0, 1)], k_all.at[pl.ds(0, 1), my_rows], 0),
-        exchange(k_send.at[pl.ds(1, steps - 1)], k_all.at[pl.ds(1, steps - 1), my_rows], 1),
-        exchange(q_send, q_all.at[:, yl], 2),
-    ]
-    for e in ex:
-        e.start()
 
     def slice_at(t, where):
         return k_all.at[t, pl.ds(pl.multiple_of(where * 2 * cols, 2 * cols), 2 * cols)]
@@ -90,12 +78,22 @@
         return pltpu.make_async_remote_copy(
             ref, ref, z_send.at[t], recv, device_id=device(zz=to), device_id_type=MESH)
 
+    mate = device(yy=1 - yl)
+
     def sign(t):
         return 1 - 2 * (t % 2)
 
     def first(t):
         for i, o in enumerate(FIRST):
-            z_copy(t, z, along_z(sign(t) * o), z_first.at[t, i]).start()
+            to = along_z(sign(t) * o)
+            own = k_all.at[t, my_rows]
+            for src, yy in ((own, yl), (k_send.at[t], 1 - yl)):
+                pltpu.make_async_remote_copy(
+                    src, own, z_send.at[t], z_first.at[t, i],
+                    device_id=device(zz=to, yy=yy), device_id_type=MESH).start()
+        pltpu.make_async_remote_copy(
+            k_send.at[t], own, z_send.at[t], z_mate.at[t],
+            device_id=mate, device_id_type=MESH).start()
 
     def relay(t):
         for i, o in enumerate(FIRST):
@@ -104,6 +102,10 @@
             for s in LEGS[o]:
                 z_copy(t, origin, along_z(sign(t) * s), z_last.at[t]).start()
 
+        @pl.when(t + AHEAD < steps)
+        def _():
+            first(t + AHEAD)
+
     def y_copy(t, yy, hh, slot, half):
         return pltpu.make_async_remote_copy(
             prod.at[t, yy], out_ref.at[x, slot], y_send.at[t], y_recv.at[t, half],
@@ -112,6 +114,7 @@
     def multiply(t):
         pltpu.make_async_copy(
             k_all.at[t, pl.ds(0, LAST * 2 * cols)], k_all.at[t, pl.ds(0, LAST * 2 * cols)], z_last.at[t]).wait()
+        pltpu.make_async_copy(k_all.at[t, my_rows], k_all.at[t, my_rows], z_mate.at[t]).wait()
         product = lax.dot_general(
             q_all[t].reshape(2 * rows, NOPE), k_all[t], (((1,), (1,)), ((), ())),
             preferred_element_type=jnp.float32)
@@ -162,13 +165,22 @@
         for half in range(2):
             x_copy((x + 2) % layers, slot_of(t, half), x_up, t, f_recv.at[t, half]).wait_recv()
 
-    ex[0].wait_recv()
-    first(0)
-    ex[1].wait_recv()
-    lax.fori_loop(1, steps, lambda t, _: (first(t), 0)[1], 0)
-    ex[2].wait_recv()
-
-    stages = ((relay, 0), (multiply, 3), (spread, 4), (forward, 6), (collect, 8))
+    for t in range(AHEAD):
+        first(t)
+
+    copies[2].wait()
+    q_f32[...] = q_in[...].reshape(rows * heads, NOPE).astype(jnp.float32)
+    for t in range(steps):
+        q_send[t] = q_f32[pl.ds(head_of(t, 1 - yl), rows, stride=heads), :].astype(jnp.bfloat16)
+    q_move = pltpu.make_async_remote_copy(
+        q_send, q_all.at[:, yl], ex_send, ex_recv, device_id=mate, device_id_type=MESH)
+    q_move.start()
+    for t in range(steps):
+        q_all[t, yl] = q_f32[pl.ds(head_of(t, yl), rows, stride=heads), :].astype(jnp.bfloat16)
+    copies[3].wait()
+    q_move.wait_recv()
+
+    stages = ((relay, 0), (multiply, 1), (spread, 2), (forward, 4), (collect, 6))
 
     def turn(i, _):
         for stage, lag in stages:
@@ -179,12 +191,11 @@
 
     lax.fori_loop(0, steps + stages[-1][1], turn, 0)
 
-    for e in ex:
-        e.wait_send()
+    q_move.wait_send()
 
     def drain(t, _):
-        pltpu.make_async_copy(
-            k_all.at[t, pl.ds(0, (NZ - 1) * 2 * cols)], k_all.at[t, pl.ds(0, (NZ - 1) * 2 * cols)], z_send.at[t]).wait()
+        sent = pl.ds(0, (2 * len(FIRST) + 1 + 2 * LAST) * cols)
+        pltpu.make_async_copy(k_all.at[t, sent], k_all.at[t, sent], z_send.at[t]).wait()
         y_copy(t, yl, b, 0, yl).wait_send()
 
         @pl.when(t % 4 != 0)
@@ -209,13 +220,12 @@
         kernel,
         out_shape=jax.ShapeDtypeStruct((layers, heads, rows, all_cols), bf),
         in_specs=[
-            pl.BlockSpec(memory_space=pl.ANY),
-            pl.BlockSpec(memory_space=pl.ANY),
-            pl.BlockSpec(memory_space=pltpu.VMEM),
-            pl.BlockSpec(memory_space=pltpu.SMEM),
-        ],
+            pl.BlockSpec(memory_space=pltpu.HBM)
+        ] * 4,
         out_specs=pl.BlockSpec(memory_space=pltpu.VMEM),
         scratch_shapes=[
+            pltpu.VMEM(latent_gain.shape, jnp.float32),
+            pltpu.SMEM(server_heads.shape, jnp.int32),
             pltpu.VMEM((rows, heads, NOPE), bf),
             pltpu.VMEM((cols, heads, NOPE), bf),
             pltpu.VMEM((rows * heads, NOPE), jnp.float32),
@@ -225,9 +235,10 @@
             pltpu.VMEM((steps, 2, rows, NOPE), bf),
             pltpu.VMEM((steps, all_cols, NOPE), bf),
             pltpu.VMEM((steps, 2, rows, all_cols), bf),
-            dma((2,)),
-            dma((3,)),
-            dma((3,)),
+            dma((4,)),
+            dma,
+            dma,
+            dma((steps,)),
             dma((steps,)),
             dma((steps, len(FIRST))),
             dma((steps,)),
@@ -239,7 +250,7 @@
         ],
         compiler_params=pltpu.CompilerParams(
             collective_id=0, has_side_effects=True, vmem_limit_bytes=48 << 20),
-    )(query_up, latent_up, latent_gain, server_heads)
+    )(*[pltpu.with_memory_space_constraint(a, pltpu.HBM) for a in (query_up, latent_up, latent_gain, server_heads)])
 
 
 def solution(mesh):

time: 72.7 us -> 64.7 us (0.89)
  Pallas kernels: 67.5 us -> 62.9 us
  local copies, waits for them, and re-layouts: 4.9 us -> 1.67 us
    pallas_call x1, Pallas kernels: 67.5 us -> 62.9 us  [local(): pl.pallas_call(kernel, out_shape=jax.ShapeDtypeStruct((layers, heads, row...]
    unnamed x9 -> x1, local copies, waits for them, and re-layouts: 4.9 us -> 1.67 us
where the time goes in v2:
time: 64.7 us; the launch traced here: 64.6 us
  Pallas kernels  62.9 us (97%)
  local copies, waits for them, and re-layouts  1.67 us (3%)
    pallas_call x1, Pallas kernels, local(): pl.pallas_call(kernel, out_shape=jax.ShapeDtypeStruct((layers, heads, row...  62.9 us
    unnamed x1, local copies, waits for them, and re-layouts  1.67 us

profile of v2, /device:TPU:1, one launch (start us, length us, event | category | flops | bytes accessed | tf_op | source)
XLA Modules:
  0.0 64.6 jit_solution(9968077324459121720)
XLA Ops:
  0.0 62.9 %shard_map.46 = bf16[4,16,48,512]{3,2,1,0:T(8,128)(2,1)S(1)} custom-call(bf16[1,48,16,192]{3,2,1,0:T(8,128)(2,1)} %q_hbm.1, bf16[1,16,16,256]{3,2,1,0:T(8,128)(2,1)} %k_hbm.1, f32[1,512]{1,0:T(1,128)} %gain_hbm.1, s32[64]{0:T(128)} %heads_hbm.1), custom_call_target="tpu_custom_call" | custom-call | tf_op jit(solution)/shard_map/pallas_call | solution.py:219
  62.9 1.7 %copy.6 = bf16[4,16,48,512]{3,2,1,0:T(8,128)(2,1)} copy(bf16[4,16,48,512]{3,2,1,0:T(8,128)(2,1)S(1)} %shard_map.46) | data formatting | bytes 6291456

commit v3 on v0

v3 whole, which is shorter than its diff:
```python
import jax
import jax.numpy as jnp
from jax import lax
from jax.experimental import pallas as pl
from jax.experimental.pallas import tpu as pltpu
from jax.sharding import PartitionSpec as P

MESH = pl.DeviceIdType.MESH
NOPE = 128
NZ = 16
AHEAD = 2
ORDER = ("S0 F2 N0 S1", "N1 F3 T0 n0", "S2 N2 n1 T1", "R0 f0 S3 N3", "n2 T2 r0 f1", "R1 n3 f2 T3", "r1 R2 f3 g0", "r2 R3 g1 r3", "g2 g3")
LANES = 128
NEAR = (1, 2, -1, -2)
ROOTS = (3, -3)
SECOND = ((3, 1), (3, 3), (-3, -1), (-3, -3))
THIRD = ((4, (1,)), (6, (1, 2)), (-4, (-1,)), (-6, (-1,)))
N_THIRD = sum(len(v) for _, v in THIRD)


def kernel(q_hbm, k_hbm, gain_hbm, heads_hbm, out_ref,
           gain_ref, heads_ref, q_in, k_in, q_f32, k_f32, q_send, k_send, q_all, k_all, prod,
           in_sem, q_sent, q_recv, z_send, z_near, z_root, z_second, z_third,
           y_send, y_recv, x_send, x_recv, f_recv):
    f, b, x = lax.axis_index("fsdp"), lax.axis_index("head"), lax.axis_index("rep")
    z, yl, yh, c = f // 2, f % 2, b // 2, b % 2
    layers = lax.axis_size("rep")
    rows, cols = q_in.shape[0], k_in.shape[0]
    heads = q_in.shape[1]
    pairs, quarters = prod.shape[:2]
    cube = z // (NZ // quarters)

    def device(zz=None, yy=None, hh=None, xx=None):
        return {
            "fsdp": (z if zz is None else zz) * 2 + (yl if yy is None else yy),
            "head": b if hh is None else hh,
            "rep": x if xx is None else xx,
        }

    def along_z(offset):
        return (z + offset + 2 * NZ) % NZ

    x_up, x_down = (x + 1) % layers, (x + layers - 1) % layers

    def owner(k):
        return (yh + k // 2) % 2 * 2 + (c + k % 2) % 2

    partners = [device(zz=along_z(s), yy=yy) for s in NEAR + ROOTS for yy in (yl, 1 - yl)]
    partners += [device(xx=x_up), device(xx=x_down)]
    partners += [device(yy=(yl + e) % 2, hh=owner(k)) for k in range(4) for e in range(2) if (k, e) != (0, 0)]
    barrier = pltpu.get_barrier_semaphore()
    for p in partners:
        pl.semaphore_signal(barrier, inc=1, device_id=p, device_id_type=MESH)

    copies = [
        pltpu.make_async_copy(heads_hbm, heads_ref, in_sem.at[0]),
        pltpu.make_async_copy(k_hbm.at[0, :, :, pl.ds(0, NOPE)], k_in, in_sem.at[1]),
        pltpu.make_async_copy(q_hbm.at[0, :, :, pl.ds(0, NOPE)], q_in, in_sem.at[2]),
        pltpu.make_async_copy(gain_hbm, gain_ref, in_sem.at[3]),
    ]
    for copy in copies:
        copy.start()
    copies[0].wait()
    copies[1].wait()
    k_f32[...] = k_in[...].reshape(cols * heads, NOPE).astype(jnp.float32)
    my_rows = pl.ds(pl.multiple_of(z * 2 * cols + yl * cols, cols), cols)

    def head_of(k, j, half):
        return heads_ref[owner(k) * heads + b * 4 + half * 2 + j] % heads

    for k in range(pairs):
        for j in range(2):
            k_send[k, j] = k_f32[pl.ds(head_of(k, j, 1 - yl), cols, stride=heads), :].astype(jnp.bfloat16)
            k_all[k, j, my_rows, :] = k_f32[pl.ds(head_of(k, j, yl), cols, stride=heads), :].astype(jnp.bfloat16)
    pl.semaphore_wait(barrier, len(partners))

    mate = device(yy=1 - yl)

    def sign(k):
        return 1 - 2 * (k % 2)

    def first(k):
        own = k_all.at[k, :, my_rows]

        def send(src, to, sem):
            pltpu.make_async_remote_copy(
                src, own, z_send.at[k], sem, device_id=to, device_id_type=MESH).start()

        for i, o in enumerate(ROOTS):
            to = along_z(sign(k) * o)
            send(own, device(zz=to), z_root.at[k, i])
            send(k_send.at[k], device(zz=to, yy=1 - yl), z_root.at[k, i])
        for o in NEAR:
            to = along_z(sign(k) * o)
            send(own, device(zz=to), z_near.at[k])
            send(k_send.at[k], device(zz=to, yy=1 - yl), z_near.at[k])
        send(k_send.at[k], mate, z_near.at[k])

    def z_copy(k, origin, to, recv):
        ref = k_all.at[k, :, pl.ds(pl.multiple_of(origin * 2 * cols, 2 * cols), 2 * cols)]
        return pltpu.make_async_remote_copy(
            ref, ref, z_send.at[k], recv, device_id=device(zz=to), device_id_type=MESH)

    def arrived(k, n, sem):
        ref = k_all.at[k, :, pl.ds(0, n * cols)]
        pltpu.make_async_copy(ref, ref, sem).wait()

    def second(k):
        for i, o in enumerate(ROOTS):
            arrived(k, 2, z_root.at[k, i])
            for n, (root, s) in enumerate(SECOND):
                if root == o:
                    z_copy(k, along_z(-sign(k) * o), along_z(sign(k) * s), z_second.at[k, n]).start()

    def third(k):
        for n, (o, steps) in enumerate(THIRD):
            arrived(k, 2, z_second.at[k, n])
            for s in steps:
                z_copy(k, along_z(-sign(k) * o), along_z(sign(k) * s), z_third.at[k]).start()

    def lanes(i):
        return pl.ds(pl.multiple_of((cube + i) % quarters * LANES, LANES), LANES)

    def y_copy(k, i, yy, hh, slot, half):
        return pltpu.make_async_remote_copy(
            prod.at[k, i, yy], out_ref.at[x, pl.ds(slot, 2), :, lanes(i)], y_send.at[k], y_recv.at[k, i, half],
            device_id=device(yy=yy, hh=hh), device_id_type=MESH)

    def multiply(k, i):
        for j in range(2):
            product = lax.dot_general(
                q_all[k, j].reshape(2 * rows, NOPE), k_all[k, j, lanes(i), :], (((1,), (1,)), ((), ())),
                preferred_element_type=jnp.float32)
            product = (product * gain_ref[:, lanes(i)]).astype(jnp.bfloat16)
            prod[k, i, 0, j] = product[:rows]
            prod[k, i, 1, j] = product[rows:]
        slot = b * 4 + yl * 2
        y_copy(k, i, 1 - yl, owner(k), slot, yl).start()

        if k == 0:
            out_ref[x, pl.ds(slot, 2), :, lanes(i)] = prod[k, i, yl]
        else:
            y_copy(k, i, yl, owner(k), slot, yl).start()

    def multiply_near(k):
        arrived(k, 2 * len(NEAR) + 1, z_near.at[k])
        multiply(k, 0)

    def multiply_far(k):
        arrived(k, 2 * N_THIRD, z_third.at[k])
        for i in range(1, quarters):
            multiply(k, i)

    def x_copy(layer, k, i, half, to, recv):
        ref = out_ref.at[layer, pl.ds(owner(k) * 4 + half * 2, 2), :, lanes(i)]
        return pltpu.make_async_remote_copy(
            ref, ref, x_send.at[k], recv, device_id=device(xx=to), device_id_type=MESH)

    def spread(k, i):
        def both(half):
            x_copy(x, k, i, half, x_up, x_recv.at[k, i, half, 0]).start()
            x_copy(x, k, i, half, x_down, x_recv.at[k, i, half, 1]).start()

        if k != 0:
            y_copy(k, i, yl, b, 0, yl).wait_recv()
        both(yl)
        y_copy(k, i, yl, b, 0, 1 - yl).wait_recv()
        both(1 - yl)

    def forward(k, i):
        x_copy(x_down, k, i, 0, x_up, x_recv.at[k, i, 0, 0]).wait_recv()
        x_copy(x_down, k, i, 0, x_up, f_recv.at[k, i, 0]).start()
        x_copy(x_up, k, i, 1, x_down, x_recv.at[k, i, 1, 1]).wait_recv()
        x_copy(x_up, k, i, 1, x_down, f_recv.at[k, i, 1]).start()

    def collect(k):
        for i in range(quarters):
            x_copy(x_up, k, i, 0, x_up, x_recv.at[k, i, 0, 1]).wait_recv()
            x_copy(x_down, k, i, 1, x_up, x_recv.at[k, i, 1, 0]).wait_recv()
            for half in range(2):
                x_copy((x + 2) % layers, k, i, half, x_up, f_recv.at[k, i, half]).wait_recv()

    for k in range(AHEAD):
        first(k)

    copies[2].wait()
    q_f32[...] = q_in[...].reshape(rows * heads, NOPE).astype(jnp.float32)
    q_moves = []
    for k in range(pairs):
        for j in range(2):
            q_send[k, j] = q_f32[pl.ds(head_of(k, j, 1 - yl), rows, stride=heads), :].astype(jnp.bfloat16)
        if k in (0, pairs - 1):
            part = pl.ds(min(k, 1), max(k, 1))
            q_moves.append(pltpu.make_async_remote_copy(
                q_send.at[part], q_all.at[part, :, yl], q_sent.at[min(k, 1)], q_recv.at[min(k, 1)],
                device_id=mate, device_id_type=MESH))
            q_moves[-1].start()
    for k in range(pairs):
        for j in range(2):
            q_all[k, j, yl] = q_f32[pl.ds(head_of(k, j, yl), rows, stride=heads), :].astype(jnp.bfloat16)
    copies[3].wait()
    for move in q_moves:
        move.wait_recv()

    run = {
        "F": first, "S": second, "T": third, "N": multiply_near, "R": multiply_far, "n": lambda k: spread(k, 0),
        "f": lambda k: forward(k, 0),
        "r": lambda k: [spread(k, i) for i in range(1, quarters)],
        "g": lambda k: [forward(k, i) for i in range(1, quarters)],
    }
    for step in " ".join(ORDER).split():
        run[step[0]](int(step[1]))
    for k in range(pairs):
        collect(k)

    for move in q_moves:
        move.wait_send()

    for k in range(pairs):
        arrived(k, 2 * (len(NEAR) + len(ROOTS)) + 1 + 2 * (len(SECOND) + N_THIRD), z_send.at[k])
        for _ in range(1 if k == 0 else 2):
            pltpu.make_async_copy(prod.at[k, :, 0], prod.at[k, :, 0], y_send.at[k]).wait()
        sent = out_ref.at[0, pl.ds(0, 12)]
        pltpu.make_async_copy(sent, sent, x_send.at[k]).wait()


def local(query_up, latent_up, latent_gain, server_heads):
    _, rows, heads, _ = query_up.shape
    cols = latent_up.shape[1]
    pairs = heads // 4
    layers = lax.axis_size("rep")
    all_cols = latent_gain.shape[1]
    quarters = all_cols // LANES
    bf, dma = jnp.bfloat16, pltpu.SemaphoreType.DMA
    operands = [pltpu.with_memory_space_constraint(a, pltpu.HBM)
                for a in (query_up, latent_up, latent_gain, server_heads)]
    return pl.pallas_call(
        kernel,
        out_shape=jax.ShapeDtypeStruct((layers, heads, rows, all_cols), bf),
        in_specs=[pl.BlockSpec(memory_space=pltpu.HBM)] * 4,
        out_specs=pl.BlockSpec(memory_space=pltpu.VMEM),
        scratch_shapes=[
            pltpu.VMEM(latent_gain.shape, jnp.float32),
            pltpu.SMEM(server_heads.shape, jnp.int32),
            pltpu.VMEM((rows, heads, NOPE), bf),
            pltpu.VMEM((cols, heads, NOPE), bf),
            pltpu.VMEM((rows * heads, NOPE), jnp.float32),
            pltpu.VMEM((cols * heads, NOPE), jnp.float32),
            pltpu.VMEM((pairs, 2, rows, NOPE), bf),
            pltpu.VMEM((pairs, 2, cols, NOPE), bf),
            pltpu.VMEM((pairs, 2, 2, rows, NOPE), bf),
            pltpu.VMEM((pairs, 2, all_cols, NOPE), bf),
            pltpu.VMEM((pairs, quarters, 2, 2, rows, LANES), bf),
            dma((4,)),
            dma((2,)),
            dma((2,)),
            dma((pairs,)),
            dma((pairs,)),
            dma((pairs, len(ROOTS))),
            dma((pairs, len(SECOND))),
            dma((pairs,)),
            dma((pairs,)),
            dma((pairs, quarters, 2)),
            dma((pairs,)),
            dma((pairs, quarters, 2, 2)),
            dma((pairs, quarters, 2)),
        ],
        compiler_params=pltpu.CompilerParams(
            collective_id=0, has_side_effects=True, vmem_limit_bytes=48 << 20),
    )(*operands)


def solution(mesh):
    in_specs = (P("rep", "fsdp", "head", None), P("rep", "fsdp", "head", None), P("rep", None), P())
    out_specs = P(None, "head", "fsdp", None)
    return jax.shard_map(local, mesh=mesh, in_specs=in_specs, out_specs=out_specs, check_vma=False)
```

time: 223 us -> 60 us (0.27)
  waiting for transfers between devices: 159 us -> 0 us
  Pallas kernels: 0 us -> 58.2 us
  blocking collectives: 39.4 us -> 0 us
  between operations: 13.5 us -> 0.01 us
  local copies, waits for them, and re-layouts: 8.17 us -> 1.67 us
  matrix products: 2.43 us -> 0 us
    all_gather x2 -> x0, waiting for transfers between devices: 159 us -> none  [the longest x1 116 us: absorb_heads(): lax.all_gather(key_nope, 'fsdp', axis=1, tiled=True)]
    pallas_call x0 -> x1, Pallas kernels: none -> 58.2 us  [local(): pl.pallas_call(kernel, out_shape=jax.ShapeDtypeStruct((layers, heads, row...]
    all_to_all x1 -> x0, blocking collectives: 39.4 us -> none  [local(): lax.all_to_all(sorted_blocks, 'head', split_axis=1, concat_axis=1, tiled=...]
    unnamed x2 -> x1, local copies, waits for them, and re-layouts: 4.42 us -> 1.67 us
    dot_general x1 -> x0, matrix products: 2.43 us -> none  [absorb_heads(): jnp.einsum('lrhd,lchd->lhrc', query_nope, lax.all_gather(key_nope, 'fsdp'...]
  transfers between devices with their start and end apart: 2 -> 0, of which waited for: 2 -> 0; matrix products, arithmetic and copies ran while one was open for 1% -> 0% of each run, Pallas kernels for 0% -> 0%
where the time goes in v3:
time: 60 us; the launch traced here: 59.9 us
  Pallas kernels  58.2 us (97%)
  local copies, waits for them, and re-layouts  1.67 us (3%)
    pallas_call x1, Pallas kernels, local(): pl.pallas_call(kernel, out_shape=jax.ShapeDtypeStruct((layers, heads, row...  58.2 us
    unnamed x1, local copies, waits for them, and re-layouts  1.67 us

profile of v3, /device:TPU:1, one launch (start us, length us, event | category | flops | bytes accessed | tf_op | source)
XLA Modules:
  0.0 59.9 jit_solution(18000450399227218135)
XLA Ops:
  0.0 58.2 %shard_map.46 = bf16[4,16,48,512]{3,2,1,0:T(8,128)(2,1)S(1)} custom-call(bf16[1,48,16,192]{3,2,1,0:T(8,128)(2,1)} %q_hbm.1, bf16[1,16,16,256]{3,2,1,0:T(8,128)(2,1)} %k_hbm.1, f32[1,512]{1,0:T(1,128)} %gain_hbm.1, s32[64]{0:T(128)} %heads_hbm.1), custom_call_target="tpu_custom_call" | custom-call | tf_op jit(solution)/shard_map/pallas_call | solution.py:237
  58.2 1.7 %copy.6 = bf16[4,16,48,512]{3,2,1,0:T(8,128)(2,1)} copy(bf16[4,16,48,512]{3,2,1,0:T(8,128)(2,1)S(1)} %shard_map.46) | data formatting | bytes 6291456

commit v4 on v3

--- a/solution.py
+++ b/solution.py
@@ -8,19 +8,20 @@
 MESH = pl.DeviceIdType.MESH
 NOPE = 128
 NZ = 16
-AHEAD = 2
-ORDER = ("S0 F2 N0 S1", "N1 F3 T0 n0", "S2 N2 n1 T1", "R0 f0 S3 N3", "n2 T2 r0 f1", "R1 n3 f2 T3", "r1 R2 f3 g0", "r2 R3 g1 r3", "g2 g3")
+AHEAD = 3
+ORDER = ("S0 N0 S1 N1", "n0 T0 M0 F3", "n1 S2 N2 p0", "T1 M1 R0 n2", "f0 S3 N3 p1", "r0 T2 M2 f1", "h0 n3 R1 T3", "M3 p2 f2 h1", "r1 g0 R2 p3", "f3 R3 r2 h2", "g1 r3 h3 g2", "g3")
 LANES = 128
 NEAR = (1, 2, -1, -2)
 ROOTS = (3, -3)
-SECOND = ((3, 1), (3, 3), (-3, -1), (-3, -3))
-THIRD = ((4, (1,)), (6, (1, 2)), (-4, (-1,)), (-6, (-1,)))
+SECOND = (1, 2, 3)
+THIRD = ((6, (1, 2)), (-6, (-1,)))
+N_MID = len(ROOTS) * (len(SECOND) - 1)
 N_THIRD = sum(len(v) for _, v in THIRD)
 
 
 def kernel(q_hbm, k_hbm, gain_hbm, heads_hbm, out_ref,
            gain_ref, heads_ref, q_in, k_in, q_f32, k_f32, q_send, k_send, q_all, k_all, prod,
-           in_sem, q_sent, q_recv, z_send, z_near, z_root, z_second, z_third,
+           in_sem, q_sent, q_recv, z_send, z_near, z_root, z_second, z_mid, z_third,
            y_send, y_recv, x_send, x_recv, f_recv):
     f, b, x = lax.axis_index("fsdp"), lax.axis_index("head"), lax.axis_index("rep")
     z, yl, yh, c = f // 2, f % 2, b // 2, b % 2
@@ -108,9 +109,9 @@
     def second(k):
         for i, o in enumerate(ROOTS):
             arrived(k, 2, z_root.at[k, i])
-            for n, (root, s) in enumerate(SECOND):
-                if root == o:
-                    z_copy(k, along_z(-sign(k) * o), along_z(sign(k) * s), z_second.at[k, n]).start()
+            for s in reversed(SECOND):
+                sem = z_second.at[k, i] if s == SECOND[-1] else z_mid.at[k]
+                z_copy(k, along_z(-sign(k) * o), along_z(sign(k) * s * (1 if o > 0 else -1)), sem).start()
 
     def third(k):
         for n, (o, steps) in enumerate(THIRD):
@@ -119,7 +120,9 @@
                 z_copy(k, along_z(-sign(k) * o), along_z(sign(k) * s), z_third.at[k]).start()
 
     def lanes(i):
-        return pl.ds(pl.multiple_of((cube + i) % quarters * LANES, LANES), LANES)
+        side = z % (NZ // quarters) // 2 * 2 - 1
+        shift = (0, side, -side, 2)[i]
+        return pl.ds(pl.multiple_of((cube + shift + quarters) % quarters * LANES, LANES), LANES)
 
     def y_copy(k, i, yy, hh, slot, half):
         return pltpu.make_async_remote_copy(
@@ -146,9 +149,13 @@
         arrived(k, 2 * len(NEAR) + 1, z_near.at[k])
         multiply(k, 0)
 
+    def multiply_mid(k):
+        arrived(k, 2 * N_MID, z_mid.at[k])
+        multiply(k, 1)
+
     def multiply_far(k):
         arrived(k, 2 * N_THIRD, z_third.at[k])
-        for i in range(1, quarters):
+        for i in range(2, quarters):
             multiply(k, i)
 
     def x_copy(layer, k, i, half, to, recv):
@@ -203,10 +210,11 @@
         move.wait_recv()
 
     run = {
-        "F": first, "S": second, "T": third, "N": multiply_near, "R": multiply_far, "n": lambda k: spread(k, 0),
-        "f": lambda k: forward(k, 0),
-        "r": lambda k: [spread(k, i) for i in range(1, quarters)],
-        "g": lambda k: [forward(k, i) for i in range(1, quarters)],
+        "F": first, "S": second, "T": third, "N": multiply_near, "M": multiply_mid, "R": multiply_far,
+        "n": lambda k: spread(k, 0), "p": lambda k: spread(k, 1),
+        "r": lambda k: [spread(k, i) for i in range(2, quarters)],
+        "f": lambda k: forward(k, 0), "h": lambda k: forward(k, 1),
+        "g": lambda k: [forward(k, i) for i in range(2, quarters)],
     }
     for step in " ".join(ORDER).split():
         run[step[0]](int(step[1]))
@@ -217,7 +225,7 @@
         move.wait_send()
 
     for k in range(pairs):
-        arrived(k, 2 * (len(NEAR) + len(ROOTS)) + 1 + 2 * (len(SECOND) + N_THIRD), z_send.at[k])
+        arrived(k, 2 * (len(NEAR) + len(ROOTS)) + 1 + 2 * (len(ROOTS) + N_MID + N_THIRD), z_send.at[k])
         for _ in range(1 if k == 0 else 2):
             pltpu.make_async_copy(prod.at[k, :, 0], prod.at[k, :, 0], y_send.at[k]).wait()
         sent = out_ref.at[0, pl.ds(0, 12)]
@@ -257,7 +265,8 @@
             dma((pairs,)),
             dma((pairs,)),
             dma((pairs, len(ROOTS))),
-            dma((pairs, len(SECOND))),
+            dma((pairs, len(ROOTS))),
+            dma((pairs,)),
             dma((pairs,)),
             dma((pairs,)),
             dma((pairs, quarters, 2)),

time: 60 us -> 58.9 us (0.982); the launches traced: 59.9 us -> 58.1 us
  Pallas kernels: 58.2 us -> 56.5 us
    pallas_call x1, Pallas kernels: 58.2 us -> 56.5 us  [local(): pl.pallas_call(kernel, out_shape=jax.ShapeDtypeStruct((layers, heads, row...]
where the time goes in v4:
time: 58.9 us; the launch traced here: 58.1 us
  Pallas kernels  56.5 us (96%)
  local copies, waits for them, and re-layouts  1.67 us (3%)
    pallas_call x1, Pallas kernels, local(): pl.pallas_call(kernel, out_shape=jax.ShapeDtypeStruct((layers, heads, row...  56.5 us
    unnamed x1, local copies, waits for them, and re-layouts  1.67 us

profile of v4, /device:TPU:1, one launch (start us, length us, event | category | flops | bytes accessed | tf_op | source)
XLA Modules:
  0.0 58.1 jit_solution(5987112556734654637)
XLA Ops:
  0.0 56.5 %shard_map.46 = bf16[4,16,48,512]{3,2,1,0:T(8,128)(2,1)S(1)} custom-call(bf16[1,48,16,192]{3,2,1,0:T(8,128)(2,1)} %q_hbm.1, bf16[1,16,16,256]{3,2,1,0:T(8,128)(2,1)} %k_hbm.1, f32[1,512]{1,0:T(1,128)} %gain_hbm.1, s32[64]{0:T(128)} %heads_hbm.1), custom_call_target="tpu_custom_call" | custom-call | tf_op jit(solution)/shard_map/pallas_call | solution.py:245
  56.5 1.7 %copy.6 = bf16[4,16,48,512]{3,2,1,0:T(8,128)(2,1)} copy(bf16[4,16,48,512]{3,2,1,0:T(8,128)(2,1)S(1)} %shard_map.46) | data formatting | bytes 6291456

commit v5 on v4

--- a/solution.py
+++ b/solution.py
@@ -9,7 +9,7 @@
 NOPE = 128
 NZ = 16
 AHEAD = 3
-ORDER = ("S0 N0 S1 N1", "n0 T0 M0 F3", "n1 S2 N2 p0", "T1 M1 R0 n2", "f0 S3 N3 p1", "r0 T2 M2 f1", "h0 n3 R1 T3", "M3 p2 f2 h1", "r1 g0 R2 p3", "f3 R3 r2 h2", "g1 r3 h3 g2", "g3")
+ORDER = ("S0 N0 S1 N1", "n0 T0 M0 F3", "n1 S2 N2 T1", "M1 p0 R0 n2", "f0 S3 N3 p1", "r0 T2 M2 f1", "R1 h0 n3 T3", "M3 p2 f2 h1", "r1 R2 g0 p3", "f3 R3 r2 h2", "g1 r3 h3 g2", "g3")
 LANES = 128
 NEAR = (1, 2, -1, -2)
 ROOTS = (3, -3)

time: 58.9 us -> 58 us (0.985)
  Pallas kernels: 56.5 us -> 55.8 us
    pallas_call x1, Pallas kernels: 56.5 us -> 55.8 us  [local(): pl.pallas_call(kernel, out_shape=jax.ShapeDtypeStruct((layers, heads, row...]
where the time goes in v5:
time: 58 us; the launch traced here: 57.5 us
  Pallas kernels  55.8 us (96%)
  local copies, waits for them, and re-layouts  1.67 us (3%)
    pallas_call x1, Pallas kernels, local(): pl.pallas_call(kernel, out_shape=jax.ShapeDtypeStruct((layers, heads, row...  55.8 us
    unnamed x1, local copies, waits for them, and re-layouts  1.67 us

profile of v5, /device:TPU:1, one launch (start us, length us, event | category | flops | bytes accessed | tf_op | source)
XLA Modules:
  0.0 57.5 jit_solution(2999684897392810909)
XLA Ops:
  0.0 55.8 %shard_map.46 = bf16[4,16,48,512]{3,2,1,0:T(8,128)(2,1)S(1)} custom-call(bf16[1,48,16,192]{3,2,1,0:T(8,128)(2,1)} %q_hbm.1, bf16[1,16,16,256]{3,2,1,0:T(8,128)(2,1)} %k_hbm.1, f32[1,512]{1,0:T(1,128)} %gain_hbm.1, s32[64]{0:T(128)} %heads_hbm.1), custom_call_target="tpu_custom_call" | custom-call | tf_op jit(solution)/shard_map/pallas_call | solution.py:245
  55.8 1.7 %copy.6 = bf16[4,16,48,512]{3,2,1,0:T(8,128)(2,1)} copy(bf16[4,16,48,512]{3,2,1,0:T(8,128)(2,1)S(1)} %shard_map.46) | data formatting | bytes 6291456
